TPU v7x, 128 devices: a whole 4x4x4 slice. The times are simulated.
128 devices in a mesh: dp: 32 (over x, y_hi, z), mp: 4 (over y_lo, core).
Axes of the slice: x: 4, y: 4 (y_hi: 2, y_lo: 2; y = y_hi * 2 + y_lo), z: 4, core: 2. Of those that a mesh axis runs over, the one named last changes fastest.
Arguments:
- block_input: bfloat16 [32, 512, 2048], P('dp', 'mp'), may hold values from -6 to 6
- lengths: int32 [32, 3], P('dp'), may hold values from 1 to 510, as said below
- gain_attn: float32 [2048], replicated, may hold values from 0.5 to 1.5
- gain_ffn: float32 [2048], replicated, may hold values from 0.5 to 1.5
- w_query: bfloat16 [2048, 256], P(None, 'mp'), may hold values from -0.125 to 0.125
- w_key: bfloat16 [2048, 256], P(None, 'mp'), may hold values from -0.125 to 0.125
- w_value: bfloat16 [2048, 2048], P(None, 'mp'), may hold values from -0.125 to 0.125
- w_out: bfloat16 [2048, 2048], P('mp'), may hold values from -0.5 to 0.5
- w_gate: bfloat16 [2048, 5504], P(None, 'mp'), may hold values from -0.125 to 0.125
- w_up: bfloat16 [2048, 5504], P(None, 'mp'), may hold values from -0.125 to 0.125
- w_down: bfloat16 [5504, 2048], P('mp'), may hold values from -0.078125 to 0.078125
- cotangent: bfloat16 [32, 512, 2048], P('dp', 'mp'), may hold values from -6 to 6
Outputs:
- block_output: bfloat16 [32, 512, 2048], P('dp', 'mp')
- grad_input: float32 [32, 512, 2048], P('dp', 'mp')
- grad_gain_attn: float32 [2048], P(('dp', 'mp'))
- grad_gain_ffn: float32 [2048], P(('dp', 'mp'))
- grad_query: float32 [2048, 256], P('dp', 'mp')
- grad_key: float32 [2048, 256], P('dp', 'mp')
- grad_value: float32 [2048, 2048], P('dp', 'mp')
- grad_out: float32 [2048, 2048], P('mp', 'dp')
- grad_gate: float32 [2048, 5504], P('dp', 'mp')
- grad_up: float32 [2048, 5504], P('dp', 'mp')
- grad_down: float32 [5504, 2048], P('mp', 'dp')
Inputs may be any that keep to these rules, and one draw needn't show every extreme that they name: `lengths`: each row holds three documents in order; the first and the last have 1 to 64 positions each, the middle one the rest of the row's 512 positions. Some row has first and last documents of one position each.
All inputs are finite; a program needn't handle non-finite values.
Results may differ from a plain program's by a relative error of at most 0.025.
Values may be sent and summed in bfloat16 or wider, within the bound.
A program may use at most 192 MiB of HBM per device.

v0:
```python
import jax
import jax.numpy as jnp
from jax import lax
from jax.sharding import PartitionSpec as P

FEAT = 16
VDIM = 128
WINDOW = 64


norm_eps = 1e-05
masked_score = -1e30


def cut_along(shard, dim, length):
    before, after = (shard.shape[:dim], shard.shape[dim + 1 :])
    return jnp.moveaxis(shard.reshape(*before, length, -1, *after), dim, 0)


def sum_at_owner(shard, axis, dim):
    length = lax.axis_size(axis)
    tiles = lax.all_to_all(cut_along(shard, dim, length), axis, 0, 0, tiled=True)
    return jnp.sum(tiles.astype(jnp.float32), axis=0)


def sent_and_summed(shard, axis, dim):
    length = lax.axis_size(axis)
    tiles = lax.all_to_all(cut_along(shard, dim, length), axis, 0, 0, tiled=True)
    return jnp.sum(tiles, axis=0)


def sent_together(arrays, axis, dim, along):
    ends, at = ([], 0)
    for a in arrays[:-1]:
        at += a.shape[along]
        ends.append(at)
    both = jnp.concatenate(arrays, axis=along)
    return tuple(
        jnp.split(lax.psum_scatter(both, axis, scatter_dimension=dim, tiled=True), ends, axis=along)
    )


def rms_scale(values, gain_vec):
    return (
        values * lax.rsqrt(jnp.mean(values * values, axis=-1, keepdims=True) + norm_eps) * gain_vec
    )


def norm_back(values, gain_vec, grad_in):
    inverse = lax.rsqrt(jnp.mean(values * values, axis=-1, keepdims=True) + norm_eps)
    unit_rows = values * inverse
    d_unit = grad_in * gain_vec
    d_values = inverse * (d_unit - unit_rows * jnp.mean(d_unit * unit_rows, axis=-1, keepdims=True))
    return (d_values, jnp.sum(grad_in * unit_rows, axis=0))


def doc_numbers(lengths, seq_len):
    doc_ends = jnp.cumsum(lengths[0])
    positions = jnp.arange(seq_len, dtype=jnp.int32)
    return jnp.sum((positions[:, None] >= doc_ends[None, :]).astype(jnp.int32), axis=1)


def block_scores(q_block, key_rows, blk_start, doc_ids):
    blk_size = q_block.shape[1]
    seq_len = key_rows.shape[0]
    raw_score = jnp.einsum("htf,shf->hts", q_block, key_rows, preferred_element_type=jnp.float32)
    rows_at = blk_start + jnp.arange(blk_size, dtype=jnp.int32)
    cols_at = jnp.arange(seq_len, dtype=jnp.int32)
    causal = (rows_at[:, None] >= cols_at[None, :]) & (doc_ids[:, None] == doc_ids[None, :])
    window = causal & (rows_at[:, None] - cols_at[None, :] < WINDOW)
    feat_scale = FEAT ** (-0.5)
    kernel = jnp.where(
        causal[None], 1.0 + raw_score * feat_scale + raw_score * raw_score * (0.5 / FEAT), 0.0
    )
    scores = jnp.where(window[None], raw_score * feat_scale, masked_score)
    return (raw_score, kernel, scores, causal)


def mixer_block(q_block, blk_start, key_rows, value_rows, doc_ids):
    raw_score, kernel, scores, causal = block_scores(q_block, key_rows, blk_start, doc_ids)
    denominator = jnp.sum(kernel, axis=2)
    numerator = jnp.einsum(
        "hts,shv->htv", kernel.astype(jnp.bfloat16), value_rows, preferred_element_type=jnp.float32
    )
    row_top = jnp.max(scores, axis=2, keepdims=True)
    weights = jnp.exp(scores - row_top)
    row_total = jnp.sum(weights, axis=2, keepdims=True)
    probs_low = (weights / row_total).astype(jnp.bfloat16)
    windowed = jnp.einsum("hts,shv->htv", probs_low, value_rows, preferred_element_type=jnp.float32)
    mixed_out = (numerator / denominator[:, :, None] + windowed).astype(jnp.bfloat16)
    return (mixed_out, denominator, (row_top + jnp.log(row_total))[:, :, 0])


def mixer_block_back(carry, inputs, key_rows, value_rows, doc_ids):
    d_keys, d_values = carry
    q_block, blk_start, d_block, denominator, log_total = inputs
    raw_score, kernel, scores, causal = block_scores(q_block, key_rows, blk_start, doc_ids)
    feat_scale = FEAT ** (-0.5)
    kernel_low = kernel.astype(jnp.bfloat16)
    numerator = jnp.einsum(
        "hts,shv->htv", kernel_low, value_rows, preferred_element_type=jnp.float32
    )
    linear = numerator / denominator[:, :, None]
    probs = jnp.exp(scores - log_total[:, :, None])
    d_mix = d_block.astype(jnp.float32)
    d_numer = (d_mix / denominator[:, :, None]).astype(jnp.bfloat16)
    d_denom = -jnp.sum(d_mix * linear, axis=2) / denominator
    d_kernel = (
        jnp.einsum("htv,shv->hts", d_numer, value_rows, preferred_element_type=jnp.float32)
        + d_denom[:, :, None]
    )
    d_probs = jnp.einsum("htv,shv->hts", d_block, value_rows, preferred_element_type=jnp.float32)
    d_scores = probs * (d_probs - jnp.sum(d_probs * probs, axis=2, keepdims=True))
    d_raw = (
        jnp.where(causal[None], d_kernel * (feat_scale + raw_score / FEAT), 0.0)
        + d_scores * feat_scale
    )
    d_raw_low = d_raw.astype(jnp.bfloat16)
    d_query = jnp.einsum(
        "hts,shf->htf", d_raw_low, key_rows, preferred_element_type=jnp.float32
    ).astype(jnp.bfloat16)
    d_keys = d_keys + jnp.einsum(
        "hts,htf->shf", d_raw_low, q_block, preferred_element_type=jnp.float32
    )
    d_values = d_values + jnp.einsum(
        "hts,htv->shv", kernel_low, d_numer, preferred_element_type=jnp.float32
    )
    d_values = d_values + jnp.einsum(
        "hts,htv->shv", probs.astype(jnp.bfloat16), d_block, preferred_element_type=jnp.float32
    )
    return ((d_keys, d_values), d_query)


def on_device(
    block_input,
    lengths,
    gain_attn,
    gain_ffn,
    w_query,
    w_key,
    w_value,
    w_out,
    w_gate,
    w_up,
    w_down,
    cotangent,
):
    model_width = block_input.shape[-1]
    own_rows = block_input.reshape(-1, model_width).astype(jnp.float32)
    tok_count = own_rows.shape[0]
    heads_here = w_query.shape[1] // FEAT
    normed = rms_scale(own_rows, gain_attn).astype(jnp.bfloat16)
    gathered = lax.all_gather(normed, "mp", axis=0, tiled=True)
    seq_len = gathered.shape[0]
    blk_size = min(512, seq_len)
    blk_count = seq_len // blk_size
    query = jnp.dot(gathered, w_query, preferred_element_type=jnp.float32).astype(jnp.bfloat16)
    key_rows = (
        jnp.dot(gathered, w_key, preferred_element_type=jnp.float32)
        .astype(jnp.bfloat16)
        .reshape(seq_len, heads_here, FEAT)
    )
    value_rows = (
        jnp.dot(gathered, w_value, preferred_element_type=jnp.float32)
        .astype(jnp.bfloat16)
        .reshape(seq_len, heads_here, VDIM)
    )
    doc_ids = doc_numbers(lengths, seq_len)
    q_blocks = jnp.transpose(query.reshape(blk_count, blk_size, heads_here, FEAT), (0, 2, 1, 3))
    blk_starts = jnp.arange(blk_count, dtype=jnp.int32) * blk_size

    def forward_block(packed):
        return mixer_block(packed[0], packed[1], key_rows, value_rows, doc_ids)

    mixed_blocks, den_blocks, lse_blocks = lax.map(forward_block, (q_blocks, blk_starts))
    mixed_flat = jnp.transpose(mixed_blocks, (0, 2, 1, 3)).reshape(seq_len, heads_here * VDIM)
    attn_out = lax.psum_scatter(
        jnp.dot(mixed_flat, w_out, preferred_element_type=jnp.float32),
        "mp",
        scatter_dimension=0,
        tiled=True,
    )
    hidden_one = own_rows + attn_out
    normed_two = rms_scale(hidden_one, gain_ffn).astype(jnp.bfloat16)
    gathered_two = lax.all_gather(normed_two, "mp", axis=0, tiled=True)
    gate_pre = jnp.dot(gathered_two, w_gate, preferred_element_type=jnp.float32)
    up_pre = jnp.dot(gathered_two, w_up, preferred_element_type=jnp.float32)
    gate_sig = jax.nn.sigmoid(gate_pre)
    gate_silu = gate_pre * gate_sig
    act_low = (gate_silu * up_pre).astype(jnp.bfloat16)
    ffn_out = sum_at_owner(
        jnp.dot(act_low, w_down, preferred_element_type=jnp.float32).astype(jnp.bfloat16), "mp", 0
    )
    block_output = (hidden_one + ffn_out).astype(jnp.bfloat16).reshape(block_input.shape)
    grad_own = cotangent.reshape(tok_count, model_width)
    grad_all = lax.all_gather(grad_own, "mp", axis=0, tiled=True)
    d_act = jnp.einsum("td,fd->tf", grad_all, w_down, preferred_element_type=jnp.float32)
    d_gate = (d_act * up_pre * (gate_sig * (1.0 + gate_pre * (1.0 - gate_sig)))).astype(
        jnp.bfloat16
    )
    d_up = (d_act * gate_silu).astype(jnp.bfloat16)
    down_part = jnp.einsum("td,tf->df", grad_all, act_low, preferred_element_type=jnp.float32)
    gate_part = jnp.einsum("td,tf->df", gathered_two, d_gate, preferred_element_type=jnp.float32)
    up_part = jnp.einsum("td,tf->df", gathered_two, d_up, preferred_element_type=jnp.float32)
    d_normed_two = lax.psum_scatter(
        jnp.einsum("tf,df->td", d_gate, w_gate, preferred_element_type=jnp.float32)
        + jnp.einsum("tf,df->td", d_up, w_up, preferred_element_type=jnp.float32),
        "mp",
        scatter_dimension=0,
        tiled=True,
    )
    d_from_norm, d_gain_ffn = norm_back(hidden_one, gain_ffn, d_normed_two)
    d_hidden = grad_own.astype(jnp.float32) + d_from_norm
    d_attn = d_hidden.astype(jnp.bfloat16)
    d_attn_all = lax.all_gather(d_attn, "mp", axis=0, tiled=True)
    out_part = jnp.einsum("td,tv->dv", d_attn_all, mixed_flat, preferred_element_type=jnp.float32)
    d_mixed = jnp.einsum("td,vd->tv", d_attn_all, w_out, preferred_element_type=jnp.float32).astype(
        jnp.bfloat16
    )
    d_mixed_blocks = jnp.transpose(
        d_mixed.reshape(blk_count, blk_size, heads_here, VDIM), (0, 2, 1, 3)
    )

    def backward_block(carry, inputs):
        return mixer_block_back(carry, inputs, key_rows, value_rows, doc_ids)

    start_carry = (
        jnp.zeros((seq_len, heads_here, FEAT), jnp.float32),
        jnp.zeros((seq_len, heads_here, VDIM), jnp.float32),
    )
    (d_keys, d_values), d_q_blocks = lax.scan(
        backward_block, start_carry, (q_blocks, blk_starts, d_mixed_blocks, den_blocks, lse_blocks)
    )
    d_query = jnp.transpose(d_q_blocks, (0, 2, 1, 3)).reshape(seq_len, heads_here * FEAT)
    d_key = d_keys.reshape(seq_len, heads_here * FEAT).astype(jnp.bfloat16)
    d_value = d_values.reshape(seq_len, heads_here * VDIM).astype(jnp.bfloat16)
    query_part = jnp.einsum("td,tf->df", gathered, d_query, preferred_element_type=jnp.float32)
    key_part = jnp.einsum("td,tf->df", gathered, d_key, preferred_element_type=jnp.float32)
    value_part = jnp.einsum("td,tf->df", gathered, d_value, preferred_element_type=jnp.float32)
    total_rows = jnp.einsum("tf,df->td", d_query, w_query, preferred_element_type=jnp.float32)
    total_rows = total_rows + jnp.einsum(
        "tf,df->td", d_key, w_key, preferred_element_type=jnp.float32
    )
    d_normed = sent_and_summed(
        total_rows + jnp.einsum("tf,df->td", d_value, w_value, preferred_element_type=jnp.float32),
        "mp",
        0,
    )
    d_from_input, d_gain_attn = norm_back(own_rows, gain_attn, d_normed)
    grad_input = (d_hidden + d_from_input).reshape(block_input.shape)
    grad_query, grad_key, grad_value, out_summed, grad_gate, grad_up, down_summed = tuple(
        (
            part.astype(jnp.float32)
            for part in sent_together(
                (
                    query_part.astype(jnp.bfloat16),
                    key_part.astype(jnp.bfloat16),
                    value_part.astype(jnp.bfloat16),
                    out_part.astype(jnp.bfloat16),
                    gate_part.astype(jnp.bfloat16),
                    up_part.astype(jnp.bfloat16),
                    down_part.astype(jnp.bfloat16),
                ),
                "dp",
                0,
                1,
            )
        )
    )
    grad_gain_attn, grad_gain_ffn = (
        lax.psum_scatter(d_gain_attn, ("dp", "mp"), scatter_dimension=0, tiled=True),
        lax.psum_scatter(d_gain_ffn, ("dp", "mp"), scatter_dimension=0, tiled=True),
    )
    return (
        block_output,
        grad_input,
        grad_gain_attn,
        grad_gain_ffn,
        grad_query,
        grad_key,
        grad_value,
        out_summed.T,
        grad_gate,
        grad_up,
        down_summed.T,
    )


def solution(mesh):
    return jax.shard_map(
        on_device,
        mesh=mesh,
        in_specs=(
            P("dp", "mp", None),
            P("dp", None),
            P(),
            P(),
            P(None, "mp"),
            P(None, "mp"),
            P(None, "mp"),
            P("mp", None),
            P(None, "mp"),
            P(None, "mp"),
            P("mp", None),
            P("dp", "mp", None),
        ),
        out_specs=(
            P("dp", "mp", None),
            P("dp", "mp", None),
            P(("dp", "mp")),
            P(("dp", "mp")),
            P("dp", "mp"),
            P("dp", "mp"),
            P("dp", "mp"),
            P("mp", "dp"),
            P("dp", "mp"),
            P("dp", "mp"),
            P("mp", "dp"),
        ),
        check_vma=False,
    )
```

profile of v0, /device:TPU:1, one launch (start us, length us, event | category | flops | bytes accessed | tf_op | source)
XLA Modules:
  0.0 689.8 jit_solution(17244073094959522326)
XLA Ops:
  7.3 1.4 fusion.60
  8.7 2.0 fusion.53
  12.0 31.6 %all-gather.6.cloned.1.call-done = bf16[512,2048]{1,0:T(8,128)(2,1)} async-done(((bf16[128,2048]{1,0:T(8,128)(2,1)}), bf16[512,2048]{1,0:T(8,128)(2,1)}) %all-gather.6.cloned.1.call-update) | async-done | bytes 2097168 | tf_op jit(solution)/shard_map/all_gather | solution.py:153
  43.6 2.3 convolution_convert_fusion.10
  46.0 2.3 convolution_convert_fusion.11
  49.3 1.8 fusion.6
  52.7 1.4 convolution_divide_fusion
  54.1 1.5 fusion.43
  55.7 3.3 fusion.89
  59.0 46.2 %reduce-scatter.6.cloned.1.call-done = f32[128,2048]{1,0:T(8,128)} async-done(((f32[512,2048]{1,0:T(8,128)}), f32[128,2048]{1,0:T(8,128)}) %reduce-scatter.6.cloned.1.call-update) | async-done | bytes 1048592 | tf_op jit(solution)/shard_map/reduce_scatter | solution.py:177
  105.2 1.6 multiply_reduce_fusion.3
  109.4 29.3 %all-gather.8.cloned.1.call-done = bf16[512,2048]{1,0:T(8,128)(2,1)} async-done(((bf16[128,2048]{1,0:T(8,128)(2,1)}), bf16[512,2048]{1,0:T(8,128)(2,1)}) %all-gather.8.cloned.1.call-update) | async-done | bytes 2097168 | tf_op jit(solution)/shard_map/all_gather | solution.py:185
  138.6 8.1 %fusion.91 = f32[512,1376]{0,1:T(8,128)} fusion(bf16[512,2048]{1,0:T(8,128)(2,1)} %all-gather.8.cloned.1.call-done, bf16[2048,1376]{0,1:T(8,128)(2,1)} %param.21), kind=kOutput, calls=%fused_computation.123 | convolution fusion | flops 2885681152 | bytes 10551296 | tf_op jit(solution)/shard_map/dot_general | solution.py:187
  146.8 7.3 %fusion.90 = f32[512,1376]{0,1:T(8,128)} fusion(bf16[512,2048]{1,0:T(8,128)(2,1)S(1)} %copy-done.39, bf16[2048,1376]{0,1:T(8,128)(2,1)} %param.20), kind=kOutput, calls=%fused_computation.122 | convolution fusion | flops 2885681152 | bytes 10551296 | tf_op jit(solution)/shard_map/dot_general | solution.py:186
  154.1 16.2 %all-gather.12.cloned.1.call-done = bf16[1,512,2048]{2,1,0:T(8,128)(2,1)} async-done(((bf16[1,128,2048]{2,1,0:T(8,128)(2,1)}), bf16[1,512,2048]{2,1,0:T(8,128)(2,1)}) %all-gather.12.cloned.1.call-update) | async-done | bytes 2097168 | tf_op jit(solution)/shard_map/all_gather | solution.py:196
  170.3 10.3 %multiply_convert_fusion = (bf16[512,1376]{0,1:T(8,128)(2,1)S(1)}, bf16[512,1376]{0,1:T(8,128)(2,1)S(1)}, bf16[512,1376]{0,1:T(8,128)(2,1)}) fusion(f32[512,1376]{0,1:T(8,128)} %fusion.90, f32[512,1376]{0,1:T(8,128)} %fusion.91, bf16[1376,2048]{1,0:T(8,128)(2,1)} %param.22, bf16[1,512,2048]{2,1,0:T(8,128)(2,1)} %all-gather.12.cloned.1.call-done), kind=kOutput, calls=%fused_computation.27 | convolution fusion | flops 2896248832 | bytes 17596416 | tf_op jit(solution)/shard_map/td,fd->tf/dot_general | solution.py:197
  180.6 6.7 fusion.92
  187.4 5.0 convolution_add_fusion
  192.5 46.2 %reduce-scatter.8.cloned.1.call-done = f32[128,2048]{1,0:T(8,128)} async-done(((f32[512,2048]{1,0:T(8,128)}), f32[128,2048]{1,0:T(8,128)}) %reduce-scatter.8.cloned.1.call-update) | async-done | bytes 1048592 | tf_op jit(solution)/shard_map/reduce_scatter | solution.py:205
  238.7 2.2 multiply_reduce_fusion.1
  241.3 2.5 fusion.83
  243.9 30.3 %all-gather.10.cloned.1.call-done = bf16[512,2048]{1,0:T(8,128)(2,1)} async-done(((bf16[128,2048]{1,0:T(8,128)(2,1)}), bf16[512,2048]{1,0:T(8,128)(2,1)}) %all-gather.10.cloned.1.call-update) | async-done | bytes 2097168 | tf_op jit(solution)/shard_map/all_gather | solution.py:215
  274.2 3.2 fusion.52
  277.5 2.9 fusion.81
  280.4 2.8 fusion.93
  283.2 2.3 fusion.18
  285.5 11.5 %fusion.45 = bf16[4,512,16]{1,2,0:T(8,128)(2,1)} fusion(bf16[512,4,16]{0,2,1:T(8,128)(2,1)S(1)} %bitcast.138, f32[4,512,512]{1,2,0:T(8,128)} %fusion.93, f32[4,512,512]{1,2,0:T(8,128)} %copy-done.4, f32[4,512,512]{1,2,0:T(8,128)} %fusion.81, f32[4,512]{1,0:T(4,128)S(1)} %get-tuple-element.129, f32[4,512]{1,0:T(4,128)S(1)} %get-tuple-element.130, ...), kind=kOutput, calls=%fused_computation.69 | convolution fusion | flops 51415552 | bytes 13254656 | tf_op jit(solution)/shard_map/while/body/eval_jaxpr/hts,shf->htf/dot_general | solution.py:119
  297.0 9.2 %fusion.48 = bf16[4,16,512]{2,1,0:T(8,128)(2,1)S(1)} fusion(bf16[4,512,16]{1,2,0:T(8,128)(2,1)S(1)} %bitcast.136, f32[4,512,512]{1,2,0:T(8,128)} %fusion.93, f32[4,512,512]{1,2,0:T(8,128)} %copy-done.4, f32[4,512,512]{1,2,0:T(8,128)} %fusion.81, f32[4,512]{1,0:T(4,128)S(1)} %get-tuple-element.129, f32[4,512]{1,0:T(4,128)S(1)} %get-tuple-element.130, ...), kind=kOutput, calls=%fused_computation.70 | convolution fusion | flops 51415552 | bytes 13254656 | tf_op jit(solution)/shard_map/while/body/eval_jaxpr/hts,htf->shf/dot_general | solution.py:122
  306.3 4.1 fusion.44
  312.8 2.6 fusion.12
  315.4 2.7 fusion.11
  318.1 4.9 fusion.2
  323.0 5.0 fusion.1
  327.9 4.9 fusion.4
  332.8 27.1 %copy.88 = bf16[2048,5280]{1,0:T(8,128)(2,1)} copy(bf16[2048,5280]{0,1:T(8,128)(2,1)} %fusion.4) | data formatting | bytes 43253760
  361.3 7.2 %convolution_convert_fusion.5 = bf16[512,2048]{1,0:T(8,128)(2,1)} fusion(bf16[512,1376]{0,1:T(8,128)(2,1)S(1)} %copy-done.47, bf16[1376,2048]{1,0:T(8,128)(2,1)} %param.22), kind=kOutput, calls=%fused_computation.26 | convolution fusion | flops 2886729728 | bytes 9142272 | tf_op jit(solution)/shard_map/dot_general | solution.py:192
  368.6 4.2 all-to-all-start
  375.8 2.8 add_add_fusion
  378.5 26.3 %all-to-all-done = bf16[4,128,2048]{2,1,0:T(8,128)(2,1)S(1)} async-done(((bf16[4,128,2048]{2,1,0:T(8,128)(2,1)}), bf16[4,128,2048]{2,1,0:T(8,128)(2,1)S(1)}, u32[]{:S(2)}, u32[]{:S(2)}) %all-to-all-start) | async-done | bytes 2097184 | tf_op jit(solution)/shard_map/all_to_all | solution.py:22
  404.8 1.3 copy-done.8
  406.2 5.3 all-to-all-start.1
  411.5 3.1 convert_reduce_fusion
  414.6 61.2 %all-to-all-done.1 = f32[4,128,2048]{2,1,0:T(8,128)} async-done(((f32[4,128,2048]{2,1,0:T(8,128)}), f32[4,128,2048]{2,1,0:T(8,128)}, u32[]{:S(2)}, u32[]{:S(2)}) %all-to-all-start.1) | async-done | bytes 4194336 | tf_op jit(solution)/shard_map/all_to_all | solution.py:28
  475.8 2.6 reduce_sum.138
  479.5 70.8 %all-reduce.2 = (f32[2048]{0:T(1024)S(1)}, f32[2048]{0:T(1024)S(1)}) all-reduce(f32[2048]{0:T(1024)S(1)} %get-tuple-element.105, f32[2048]{0:T(1024)S(1)} %copy-done.30), channel_id=5, replica_groups=mesh['dp'=32,'mp'=4] {'dp','mp'}, use_global_device_ids=true, to_apply=%region_16.17.clone | all-reduce | flops 4096 | bytes 32768
  551.4 4.0 fusion.58
  555.4 115.5 %reduce-scatter.10.cloned.1.call-done = bf16[64,5280]{1,0:T(8,128)(2,1)} async-done(((bf16[2048,5280]{1,0:T(8,128)(2,1)}), bf16[64,5280]{1,0:T(8,128)(2,1)}) %reduce-scatter.10.cloned.1.call-update) | async-done | bytes 675856
  676.1 1.9 fusion.86
  (150 shorter events, 25.6 us)
Async XLA Ops:
  7.2 48.5 %copy-start = (bf16[512,2048]{1,0:T(8,128)(2,1)S(1)}, bf16[512,2048]{1,0:T(8,128)(2,1)}, u32[]{:S(2)}) copy-start(bf16[512,2048]{1,0:T(8,128)(2,1)} %param.19) | copy-start | bytes 6291460
  7.2 38.8 %copy-start.18 = (bf16[2048,64]{0,1:T(8,128)(2,1)S(1)}, bf16[2048,64]{0,1:T(8,128)(2,1)}, u32[]{:S(2)}) copy-start(bf16[2048,64]{0,1:T(8,128)(2,1)} %param.16) | copy-start | bytes 786436
  7.2 36.4 %all-gather.6.cloned.1.call-start = ((), (), s32[]{:S(2)}) async-start(), calls=%async_computation.5 | async-start | bytes 2621440 | tf_op jit(solution)/shard_map/all_gather | solution.py:153
  8.7 2.9 copy-start.35
  10.7 94.5 %reduce-scatter.6.cloned.1.call-start = ((), (), s32[]{:S(2)}) async-start(), calls=%async_computation.6 | async-start | bytes 5242880 | tf_op jit(solution)/shard_map/reduce_scatter | solution.py:177
  12.0 40.7 %copy-start.21 = (pred[512,512]{0,1:T(8,128)(4,1)}, pred[512,512]{0,1:T(8,128)(4,1)S(1)}, u32[]{:S(2)}) copy-start(pred[512,512]{0,1:T(8,128)(4,1)S(1)} %get-tuple-element.123) | copy-start | bytes 786436
  48.3 2.8 copy-start.2
  48.4 3.0 copy-start.12
  49.3 4.8 copy-start.4
  49.3 4.8 copy-start.28
  51.4 2.7 copy-start.31
  55.6 3.3 copy-start.23
  58.9 48.4 %copy-start.26 = (f32[2048]{0:T(1024)S(1)}, f32[2048]{0:T(1024)}, u32[]{:S(2)}) copy-start(f32[2048]{0:T(1024)} %param.15) | copy-start | bytes 24580
  59.0 79.7 %all-gather.8.cloned.1.call-start = ((), (), s32[]{:S(2)}) async-start(), calls=%async_computation.7 | async-start | bytes 2621440 | tf_op jit(solution)/shard_map/all_gather | solution.py:185
  108.3 62.0 %all-gather.12.cloned.1.call-start = ((), (), s32[]{:S(2)}) async-start(), calls=%async_computation.10 | async-start | bytes 2621440 | tf_op jit(solution)/shard_map/all_gather | solution.py:196
  108.9 129.8 %reduce-scatter.8.cloned.1.call-start = ((), (), s32[]{:S(2)}) async-start(), calls=%async_computation.8 | async-start | bytes 5242880 | tf_op jit(solution)/shard_map/reduce_scatter | solution.py:205
  138.6 8.1 %copy-start.39 = (bf16[512,2048]{1,0:T(8,128)(2,1)S(1)}, bf16[512,2048]{1,0:T(8,128)(2,1)}, u32[]{:S(2)}) copy-start(bf16[512,2048]{1,0:T(8,128)(2,1)} %all-gather.8.cloned.1.call-done) | copy-start | bytes 6291460
  180.6 6.8 copy-start.43
  180.6 6.8 copy-start.14
  180.6 6.8 slice-start
  180.6 6.8 slice-start.1
  192.4 81.8 %all-gather.10.cloned.1.call-start = ((), (), s32[]{:S(2)}) async-start(), calls=%async_computation.9 | async-start | bytes 2621440 | tf_op jit(solution)/shard_map/all_gather | solution.py:215
  243.8 427.1 %reduce-scatter.10.cloned.1.call-start = ((), (), s32[]{:S(2)}) async-start(), calls=%async_computation.11 | async-start | bytes 22708224
  274.2 3.2 copy-start.10
  277.4 5.8 copy-start.11
  277.4 5.7 copy-start.29
  277.5 5.7 copy-start.32
  277.5 5.7 copy-start.5
  306.2 4.1 copy-start.3
  306.2 4.1 copy-start.25
  310.3 5.1 copy-start.16
  311.6 3.8 copy-start.24
  311.6 3.8 copy-start.42
  315.4 2.7 copy-start.40
  315.4 2.7 copy-start.44
  318.1 4.9 copy-start.15
  323.0 5.0 copy-start.41
  323.0 5.0 copy-start.46
  368.6 4.2 copy-start.19
  368.6 36.3 %all-to-all-start = ((bf16[4,128,2048]{2,1,0:T(8,128)(2,1)}), bf16[4,128,2048]{2,1,0:T(8,128)(2,1)S(1)}, u32[]{:S(2)}, u32[]{:S(2)}) async-start(bf16[4,128,2048]{2,1,0:T(8,128)(2,1)} %bitcast.130), calls=%async_computation.1 | async-start | bytes 4194304 | tf_op jit(solution)/shard_map/all_to_all | solution.py:22
  406.2 69.6 %all-to-all-start.1 = ((f32[4,128,2048]{2,1,0:T(8,128)}), f32[4,128,2048]{2,1,0:T(8,128)}, u32[]{:S(2)}, u32[]{:S(2)}) async-start(f32[4,128,2048]{2,1,0:T(8,128)} %bitcast.119), calls=%async_computation.3 | async-start | bytes 8388608 | tf_op jit(solution)/shard_map/all_to_all | solution.py:28
  411.5 67.0 %copy-start.6 = (bf16[1,128,2048]{2,1,0:T(8,128)(2,1)S(1)}, bf16[1,128,2048]{2,1,0:T(8,128)(2,1)}, u32[]{:S(2)}) copy-start(bf16[1,128,2048]{2,1,0:T(8,128)(2,1)} %param.12) | copy-start | bytes 1572868
  411.5 67.0 %copy-start.27 = (f32[2048]{0:T(1024)S(1)}, f32[2048]{0:T(1024)}, u32[]{:S(2)}) copy-start(f32[2048]{0:T(1024)} %param.14) | copy-start | bytes 24580
  411.5 67.0 %copy-start.36 = (f32[128]{0:T(128)S(1)}, f32[128]{0:T(128)}, u32[]{:S(2)}) copy-start(f32[128]{0:T(128)} %copy-done.35) | copy-start | bytes 1540
  414.6 64.8 %copy-start.30 = (f32[2048]{0:T(1024)S(1)}, f32[2048]{0:T(1024)}, u32[]{:S(2)}) copy-start(f32[2048]{0:T(1024)} %get-tuple-element.103) | copy-start | bytes 24580
  414.6 136.8 %copy-start.34 = (f32[128]{0:T(128)S(1)}, f32[128]{0:T(128)}, u32[]{:S(2)}) copy-start(f32[128]{0:T(128)} %copy-done.33) | copy-start | bytes 1540
  414.6 136.8 %copy-start.38 = (f32[128]{0:T(128)S(1)}, f32[128]{0:T(128)}, u32[]{:S(2)}) copy-start(f32[128]{0:T(128)} %copy-done.37) | copy-start | bytes 1540
  551.4 131.0 %copy-start.1 = (bf16[512,2048]{1,0:T(8,128)(2,1)S(1)}, bf16[512,2048]{1,0:T(8,128)(2,1)}, u32[]{:S(2)}) copy-start(bf16[512,2048]{1,0:T(8,128)(2,1)} %param.19) | copy-start | bytes 6291460
  (11 other events, 14.6 us)
Sparse Core Ops, SparseCore 0:
  10.8 32.7 all-gather.5
  59.1 46.0 reduce-scatter.5
  108.4 30.1 all-gather.7
  140.3 29.9 all-gather.11
  192.5 46.0 reduce-scatter.7
  244.0 30.1 all-gather.9
  360.1 310.7 reduce-scatter.9
where the time goes:
time: 698 us; the launch traced here: 690 us
  waiting for transfers between devices  403 us (58%)
  matrix products  121 us (17%)
  blocking collectives  70.8 us (10%)
  local copies, waits for them, and re-layouts  45.4 us (7%)
  other arithmetic  23.9 us (3%)
  between operations  15.2 us (2%)
  starting transfers between devices  10.3 us (1%)
    unnamed x8, waiting for transfers between devices  116 us
    unnamed x1, blocking collectives  70.8 us
    all_to_all x1, waiting for transfers between devices, sent_and_summed(): lax.all_to_all(cut_along(shard, dim, length), axis, 0, 0, tiled=True)  61.2 us
    reduce_scatter x1, waiting for transfers between devices, on_device(): lax.psum_scatter(jnp.einsum('tf,df->td', d_gate, w_gate, preferred_elemen...  46.2 us
    reduce_scatter x1, waiting for transfers between devices, on_device(): lax.psum_scatter(jnp.dot(mixed_flat, w_out, preferred_element_type=jnp.fl...  46.2 us
    unnamed x117, local copies, waits for them, and re-layouts  41.7 us
    all_gather x1, waiting for transfers between devices, on_device(): gathered = lax.all_gather(normed, 'mp', axis=0, tiled=True)  31.6 us
    all_gather x1, waiting for transfers between devices, on_device(): d_attn_all = lax.all_gather(d_attn, 'mp', axis=0, tiled=True)  30.3 us
  transfers between devices with their start and end apart: 9, of which 9 were waited for; matrix products, arithmetic and copies ran while one was open for 6% of the time, Pallas kernels for 0%

commit v1 on v0

--- a/solution.py
+++ b/solution.py
@@ -1,7 +1,15 @@
+import functools
+
 import jax
 import jax.numpy as jnp
 from jax import lax
+from jax.experimental import pallas as pl
+from jax.experimental.pallas import tpu as pltpu
 from jax.sharding import PartitionSpec as P
+
+MESH = pl.DeviceIdType.MESH
+F32 = jnp.float32
+BF16 = jnp.bfloat16
 
 FEAT = 16
 VDIM = 128
@@ -12,32 +20,384 @@
 masked_score = -1e30
 
 
-def cut_along(shard, dim, length):
-    before, after = (shard.shape[:dim], shard.shape[dim + 1 :])
-    return jnp.moveaxis(shard.reshape(*before, length, -1, *after), dim, 0)
-
-
-def sum_at_owner(shard, axis, dim):
-    length = lax.axis_size(axis)
-    tiles = lax.all_to_all(cut_along(shard, dim, length), axis, 0, 0, tiled=True)
-    return jnp.sum(tiles.astype(jnp.float32), axis=0)
-
-
-def sent_and_summed(shard, axis, dim):
-    length = lax.axis_size(axis)
-    tiles = lax.all_to_all(cut_along(shard, dim, length), axis, 0, 0, tiled=True)
-    return jnp.sum(tiles, axis=0)
-
-
-def sent_together(arrays, axis, dim, along):
-    ends, at = ([], 0)
-    for a in arrays[:-1]:
-        at += a.shape[along]
-        ends.append(at)
-    both = jnp.concatenate(arrays, axis=along)
-    return tuple(
-        jnp.split(lax.psum_scatter(both, axis, scatter_dimension=dim, tiled=True), ends, axis=along)
-    )
+def place():
+    dp, mp = lax.axis_index("dp"), lax.axis_index("mp")
+    return dp // 8, (dp // 4) % 2, dp % 4, mp // 2, mp % 2
+
+
+def device(x, yh, z, yl, core):
+    return (x * 8 + yh * 4 + z, yl * 2 + core)
+
+
+def greet(devices):
+    barrier = pltpu.get_barrier_semaphore()
+    for target in devices:
+        pl.semaphore_signal(barrier, inc=1, device_id=target, device_id_type=MESH)
+    pl.semaphore_wait(barrier, len(devices))
+
+
+def remote(src, dst, send_sem, recv_sem, target):
+    return pltpu.make_async_remote_copy(
+        src_ref=src,
+        dst_ref=dst,
+        send_sem=send_sem,
+        recv_sem=recv_sem,
+        device_id=target,
+        device_id_type=MESH,
+    )
+
+
+PARTS = 4
+
+
+def gather_kernel(own_ref, full_ref, send, recv):
+    x, yh, z, yl, core = place()
+    mate, pair = device(x, yh, z, yl, 1 - core), device(x, yh, z, 1 - yl, core)
+    tok = own_ref.shape[0]
+    piece = tok // PARTS
+    greet((mate, pair))
+    mine, far = yl * 2 + core, (1 - yl) * 2 + core
+    outgoing = []
+    for i in range(PARTS):
+        copy = remote(
+            own_ref.at[pl.ds(i * piece, piece)],
+            full_ref.at[pl.ds(pl.multiple_of(mine * tok + i * piece, piece), piece)],
+            send.at[i],
+            recv.at[i],
+            pair,
+        )
+        copy.start()
+        outgoing.append(copy)
+    near = remote(
+        own_ref,
+        full_ref.at[pl.ds(pl.multiple_of(mine * tok, tok), tok)],
+        send.at[PARTS],
+        recv.at[PARTS],
+        mate,
+    )
+    near.start()
+    full_ref[pl.ds(pl.multiple_of(mine * tok, tok), tok), :] = own_ref[...]
+    passed = []
+    for i in range(PARTS):
+        outgoing[i].wait_recv()
+        rows = pl.ds(pl.multiple_of(far * tok + i * piece, piece), piece)
+        copy = remote(
+            full_ref.at[rows],
+            full_ref.at[rows],
+            send.at[PARTS + 1 + i],
+            recv.at[PARTS + 1 + i],
+            mate,
+        )
+        copy.start()
+        passed.append(copy)
+    near.wait()
+    for i in range(PARTS):
+        outgoing[i].wait_send()
+        passed[i].wait()
+
+
+def gather_rows(own):
+    tok, width = own.shape
+    return pl.pallas_call(
+        gather_kernel,
+        out_shape=jax.ShapeDtypeStruct((4 * tok, width), own.dtype),
+        in_specs=[pl.BlockSpec(memory_space=pltpu.VMEM)],
+        out_specs=pl.BlockSpec(memory_space=pltpu.VMEM),
+        scratch_shapes=[
+            pltpu.SemaphoreType.DMA((2 * PARTS + 1,)),
+            pltpu.SemaphoreType.DMA((2 * PARTS + 1,)),
+        ],
+        compiler_params=pltpu.CompilerParams(
+            collective_id=0, has_side_effects=True, vmem_limit_bytes=32 << 20
+        ),
+        name="gather_rows",
+    )(own)
+
+
+def scatter_kernel(part_ref, out_ref, near_out, near_in, far_out, far_in, send, recv):
+    x, yh, z, yl, core = place()
+    mate, pair = device(x, yh, z, yl, 1 - core), device(x, yh, z, 1 - yl, core)
+    tok = out_ref.shape[0]
+    piece = tok // PARTS
+    greet((mate, pair))
+    near_copies = []
+    for k, side in enumerate((1 - yl, yl)):
+        start = pl.multiple_of((side * 2 + 1 - core) * tok, tok)
+        near_out[k] = part_ref[pl.ds(start, tok), :].astype(BF16)
+        copy = remote(near_out.at[k], near_in.at[k], send.at[k], recv.at[k], mate)
+        copy.start()
+        near_copies.append(copy)
+    near_copies[0].wait_recv()
+    far_copies = []
+    far_start = pl.multiple_of(((1 - yl) * 2 + core) * tok, tok)
+    for i in range(PARTS):
+        rows = pl.ds(i * piece, piece)
+        far_out[rows] = (
+            part_ref[pl.ds(far_start + i * piece, piece), :] + near_in[0, rows].astype(F32)
+        ).astype(BF16)
+        copy = remote(far_out.at[rows], far_in.at[rows], send.at[2 + i], recv.at[2 + i], pair)
+        copy.start()
+        far_copies.append(copy)
+    near_copies[1].wait_recv()
+    own_start = pl.multiple_of((yl * 2 + core) * tok, tok)
+    for i in range(PARTS):
+        rows = pl.ds(i * piece, piece)
+        far_copies[i].wait_recv()
+        out_ref[rows, :] = (
+            part_ref[pl.ds(own_start + i * piece, piece), :]
+            + near_in[1, rows].astype(F32)
+            + far_in[rows].astype(F32)
+        )
+    for copy in near_copies + far_copies:
+        copy.wait_send()
+
+
+def scatter_rows(part):
+    rows, width = part.shape
+    tok = rows // 4
+    return pl.pallas_call(
+        scatter_kernel,
+        out_shape=jax.ShapeDtypeStruct((tok, width), F32),
+        in_specs=[pl.BlockSpec(memory_space=pltpu.VMEM)],
+        out_specs=pl.BlockSpec(memory_space=pltpu.VMEM),
+        scratch_shapes=[
+            pltpu.VMEM((2, tok, width), BF16),
+            pltpu.VMEM((2, tok, width), BF16),
+            pltpu.VMEM((tok, width), BF16),
+            pltpu.VMEM((tok, width), BF16),
+            pltpu.SemaphoreType.DMA((2 + PARTS,)),
+            pltpu.SemaphoreType.DMA((2 + PARTS,)),
+        ],
+        compiler_params=pltpu.CompilerParams(
+            collective_id=1, has_side_effects=True, vmem_limit_bytes=48 << 20
+        ),
+        name="scatter_rows",
+    )(part)
+
+
+def add_into(dst, terms, rows, step):
+    def body(i, _):
+        at = pl.ds(pl.multiple_of(i * step, step), step)
+        total = dst[at, :].astype(F32)
+        for term in terms:
+            total = total + term[at, :].astype(F32)
+        dst[at, :] = total.astype(dst.dtype)
+        return 0
+
+    lax.fori_loop(0, rows // step, body, 0)
+
+
+class RowSum:
+    def __init__(self, grad, bufs, send, recv):
+        self.grad = grad
+        self.t1, self.m1, self.t2, self.m2, self.last = bufs
+        self.send, self.recv = send, recv
+        self.x, self.yh, self.z, self.yl, self.core = place()
+
+    def near(self, path, stage, step):
+        if (path == 0) == (stage == 0):
+            return device((self.x + step + 4) % 4, self.yh, self.z, self.yl, self.core)
+        return device(self.x, self.yh, (self.z + step + 4) % 4, self.yl, self.core)
+
+    def at(self, path, stage):
+        return self.x if (path == 0) == (stage == 0) else self.z
+
+    def block(self, path, b, k):
+        return self.grad.at[b, 0, k] if path == 0 else self.grad.at[k, 1, b]
+
+    def copy(self, src, dst, path, slot, target):
+        return remote(src, dst, self.send.at[path, slot], self.recv.at[path, slot], target)
+
+    def transit_one(self, path, side):
+        b = (self.at(path, 0) + 2) % 4
+        return self.copy(
+            self.block(path, b, pl.ds(2 * side, 2)),
+            self.t1.at[path, side],
+            path,
+            side,
+            self.near(path, 0, 1 - 2 * side),
+        )
+
+    def main_one(self, path, side, half):
+        step = 1 - 2 * side
+        b = (self.at(path, 0) + step + 4) % 4
+        src = (
+            self.t1.at[path, side]
+            if half == side
+            else self.block(path, b, pl.ds(2 * half, 2))
+        )
+        return self.copy(
+            src,
+            self.m1.at[path, side, pl.ds(2 * half, 2)],
+            path,
+            2 + 2 * side + half,
+            self.near(path, 0, step),
+        )
+
+    def transit_two(self, path, side):
+        k = (self.at(path, 1) + 2) % 4
+        return self.copy(
+            self.m1.at[path, 0, k, pl.ds(32 * side, 32)],
+            self.t2.at[path, side],
+            path,
+            6 + side,
+            self.near(path, 1, 1 - 2 * side),
+        )
+
+    def main_two(self, path, side, half):
+        step = 1 - 2 * side
+        k = (self.at(path, 1) + step + 4) % 4
+        rows = pl.ds(32 * half, 32)
+        src = self.t2.at[path, side] if half == side else self.m1.at[path, 0, k, rows]
+        return self.copy(
+            src,
+            self.m2.at[path, side, rows],
+            path,
+            8 + 2 * side + half,
+            self.near(path, 1, step),
+        )
+
+    def last_copy(self):
+        target = device(self.x, 1 - self.yh, self.z, self.yl, self.core)
+        return self.copy(self.m2.at[1 - self.yh, 0], self.last, 0, 12, target)
+
+    def start_one(self):
+        for path in (0, 1):
+            for side in (0, 1):
+                self.transit_one(path, side).start()
+        for path in (0, 1):
+            for side in (0, 1):
+                self.main_one(path, side, 1 - side).start()
+
+    def pass_one(self):
+        for path in (0, 1):
+            for side in (0, 1):
+                self.transit_one(path, side).wait_recv()
+                b = (self.at(path, 0) + 1 - 2 * side + 4) % 4
+                for k in (0, 1):
+                    add_into(
+                        self.t1.at[path, side, k],
+                        (self.block(path, b, 2 * side + k),),
+                        64,
+                        16,
+                    )
+                self.main_one(path, side, side).start()
+
+    def join_one(self):
+        for path in (0, 1):
+            for side in (0, 1):
+                for half in (0, 1):
+                    self.main_one(path, side, half).wait_recv()
+            b = self.at(path, 0)
+
+            def body(k, _):
+                add_into(
+                    self.m1.at[path, 0, k],
+                    (self.m1.at[path, 1, k], self.block(path, b, k)),
+                    64,
+                    16,
+                )
+                return 0
+
+            lax.fori_loop(0, 4, body, 0)
+            for side in (0, 1):
+                self.transit_two(path, side).start()
+            for side in (0, 1):
+                self.main_two(path, side, 1 - side).start()
+
+    def pass_two(self):
+        for path in (0, 1):
+            for side in (0, 1):
+                self.transit_two(path, side).wait_recv()
+                k = (self.at(path, 1) + 1 - 2 * side + 4) % 4
+                add_into(
+                    self.t2.at[path, side],
+                    (self.m1.at[path, 0, k, pl.ds(32 * side, 32)],),
+                    32,
+                    16,
+                )
+                self.main_two(path, side, side).start()
+
+    def join_two(self):
+        for path in (0, 1):
+            for side in (0, 1):
+                for half in (0, 1):
+                    self.main_two(path, side, half).wait_recv()
+            k = self.at(path, 1)
+            add_into(self.m2.at[path, 0], (self.m2.at[path, 1], self.m1.at[path, 0, k]), 64, 16)
+        self.last_copy().start()
+
+    def finish(self, out):
+        self.last_copy().wait_recv()
+        out[...] = self.m2[self.yh, 0].astype(F32) + self.last[...].astype(F32)
+        for path in (0, 1):
+            for side in (0, 1):
+                self.transit_one(path, side).wait_send()
+                self.transit_two(path, side).wait_send()
+                for half in (0, 1):
+                    self.main_one(path, side, half).wait_send()
+                    self.main_two(path, side, half).wait_send()
+        self.last_copy().wait_send()
+
+
+def sum_buffers(width):
+    return [
+        pltpu.VMEM((2, 2, 2, 64, width), BF16),
+        pltpu.VMEM((2, 2, 4, 64, width), BF16),
+        pltpu.VMEM((2, 2, 32, width), BF16),
+        pltpu.VMEM((2, 2, 64, width), BF16),
+        pltpu.VMEM((64, width), BF16),
+        pltpu.SemaphoreType.DMA((2, 13)),
+        pltpu.SemaphoreType.DMA((2, 13)),
+    ]
+
+
+def sum_neighbours():
+    x, yh, z, yl, core = place()
+    return (
+        device((x + 1) % 4, yh, z, yl, core),
+        device((x + 3) % 4, yh, z, yl, core),
+        device(x, yh, (z + 1) % 4, yl, core),
+        device(x, yh, (z + 3) % 4, yl, core),
+        device(x, 1 - yh, z, yl, core),
+    )
+
+
+def weights_kernel(n, *refs):
+    grads, outs, scratch = refs[:n], refs[n : 2 * n], refs[2 * n :]
+    greet(sum_neighbours())
+    units = [
+        RowSum(grads[i], scratch[7 * i : 7 * i + 5], scratch[7 * i + 5], scratch[7 * i + 6])
+        for i in range(n)
+    ]
+    for u in units:
+        u.start_one()
+    for u in units:
+        u.pass_one()
+    for u in units:
+        u.join_one()
+    for u in units:
+        u.pass_two()
+    for u in units:
+        u.join_two()
+    for u, out in zip(units, outs):
+        u.finish(out)
+
+
+def sum_weights(grads):
+    n = len(grads)
+    grads = [g.reshape(4, 2, 4, 64, g.shape[-1]) for g in grads]
+    return pl.pallas_call(
+        functools.partial(weights_kernel, n),
+        out_shape=[jax.ShapeDtypeStruct((64, g.shape[-1]), F32) for g in grads],
+        in_specs=[pl.BlockSpec(memory_space=pltpu.VMEM)] * n,
+        out_specs=[pl.BlockSpec(memory_space=pltpu.VMEM)] * n,
+        scratch_shapes=[b for g in grads for b in sum_buffers(g.shape[-1])],
+        compiler_params=pltpu.CompilerParams(
+            collective_id=2, has_side_effects=True, vmem_limit_bytes=60 << 20
+        ),
+        name="sum_weights",
+    )(*grads)
 
 
 def rms_scale(values, gain_vec):
@@ -150,7 +510,7 @@
     tok_count = own_rows.shape[0]
     heads_here = w_query.shape[1] // FEAT
     normed = rms_scale(own_rows, gain_attn).astype(jnp.bfloat16)
-    gathered = lax.all_gather(normed, "mp", axis=0, tiled=True)
+    gathered = gather_rows(normed)
     seq_len = gathered.shape[0]
     blk_size = min(512, seq_len)
     blk_count = seq_len // blk_size
@@ -174,26 +534,19 @@
 
     mixed_blocks, den_blocks, lse_blocks = lax.map(forward_block, (q_blocks, blk_starts))
     mixed_flat = jnp.transpose(mixed_blocks, (0, 2, 1, 3)).reshape(seq_len, heads_here * VDIM)
-    attn_out = lax.psum_scatter(
-        jnp.dot(mixed_flat, w_out, preferred_element_type=jnp.float32),
-        "mp",
-        scatter_dimension=0,
-        tiled=True,
-    )
+    attn_out = scatter_rows(jnp.dot(mixed_flat, w_out, preferred_element_type=jnp.float32))
     hidden_one = own_rows + attn_out
     normed_two = rms_scale(hidden_one, gain_ffn).astype(jnp.bfloat16)
-    gathered_two = lax.all_gather(normed_two, "mp", axis=0, tiled=True)
+    gathered_two = gather_rows(normed_two)
     gate_pre = jnp.dot(gathered_two, w_gate, preferred_element_type=jnp.float32)
     up_pre = jnp.dot(gathered_two, w_up, preferred_element_type=jnp.float32)
     gate_sig = jax.nn.sigmoid(gate_pre)
     gate_silu = gate_pre * gate_sig
     act_low = (gate_silu * up_pre).astype(jnp.bfloat16)
-    ffn_out = sum_at_owner(
-        jnp.dot(act_low, w_down, preferred_element_type=jnp.float32).astype(jnp.bfloat16), "mp", 0
-    )
+    ffn_out = scatter_rows(jnp.dot(act_low, w_down, preferred_element_type=jnp.float32))
     block_output = (hidden_one + ffn_out).astype(jnp.bfloat16).reshape(block_input.shape)
     grad_own = cotangent.reshape(tok_count, model_width)
-    grad_all = lax.all_gather(grad_own, "mp", axis=0, tiled=True)
+    grad_all = gather_rows(grad_own)
     d_act = jnp.einsum("td,fd->tf", grad_all, w_down, preferred_element_type=jnp.float32)
     d_gate = (d_act * up_pre * (gate_sig * (1.0 + gate_pre * (1.0 - gate_sig)))).astype(
         jnp.bfloat16
@@ -202,17 +555,14 @@
     down_part = jnp.einsum("td,tf->df", grad_all, act_low, preferred_element_type=jnp.float32)
     gate_part = jnp.einsum("td,tf->df", gathered_two, d_gate, preferred_element_type=jnp.float32)
     up_part = jnp.einsum("td,tf->df", gathered_two, d_up, preferred_element_type=jnp.float32)
-    d_normed_two = lax.psum_scatter(
+    d_normed_two = scatter_rows(
         jnp.einsum("tf,df->td", d_gate, w_gate, preferred_element_type=jnp.float32)
-        + jnp.einsum("tf,df->td", d_up, w_up, preferred_element_type=jnp.float32),
-        "mp",
-        scatter_dimension=0,
-        tiled=True,
+        + jnp.einsum("tf,df->td", d_up, w_up, preferred_element_type=jnp.float32)
     )
     d_from_norm, d_gain_ffn = norm_back(hidden_one, gain_ffn, d_normed_two)
     d_hidden = grad_own.astype(jnp.float32) + d_from_norm
     d_attn = d_hidden.astype(jnp.bfloat16)
-    d_attn_all = lax.all_gather(d_attn, "mp", axis=0, tiled=True)
+    d_attn_all = gather_rows(d_attn)
     out_part = jnp.einsum("td,tv->dv", d_attn_all, mixed_flat, preferred_element_type=jnp.float32)
     d_mixed = jnp.einsum("td,vd->tv", d_attn_all, w_out, preferred_element_type=jnp.float32).astype(
         jnp.bfloat16
@@ -241,31 +591,27 @@
     total_rows = total_rows + jnp.einsum(
         "tf,df->td", d_key, w_key, preferred_element_type=jnp.float32
     )
-    d_normed = sent_and_summed(
-        total_rows + jnp.einsum("tf,df->td", d_value, w_value, preferred_element_type=jnp.float32),
-        "mp",
-        0,
+    d_normed = scatter_rows(
+        total_rows + jnp.einsum("tf,df->td", d_value, w_value, preferred_element_type=jnp.float32)
     )
     d_from_input, d_gain_attn = norm_back(own_rows, gain_attn, d_normed)
     grad_input = (d_hidden + d_from_input).reshape(block_input.shape)
-    grad_query, grad_key, grad_value, out_summed, grad_gate, grad_up, down_summed = tuple(
-        (
-            part.astype(jnp.float32)
-            for part in sent_together(
-                (
-                    query_part.astype(jnp.bfloat16),
-                    key_part.astype(jnp.bfloat16),
-                    value_part.astype(jnp.bfloat16),
-                    out_part.astype(jnp.bfloat16),
-                    gate_part.astype(jnp.bfloat16),
-                    up_part.astype(jnp.bfloat16),
-                    down_part.astype(jnp.bfloat16),
-                ),
-                "dp",
-                0,
-                1,
-            )
-        )
+    mixer_part = jnp.concatenate(
+        [query_part.astype(BF16), key_part.astype(BF16), value_part.astype(BF16)], axis=1
+    )
+    mixer_summed, out_summed, grad_gate, grad_up, down_summed = sum_weights(
+        [
+            mixer_part,
+            out_part.astype(BF16),
+            gate_part.astype(BF16),
+            up_part.astype(BF16),
+            down_part.astype(BF16),
+        ]
+    )
+    grad_query, grad_key, grad_value = (
+        mixer_summed[:, :64],
+        mixer_summed[:, 64:128],
+        mixer_summed[:, 128:],
     )
     grad_gain_attn, grad_gain_ffn = (
         lax.psum_scatter(d_gain_attn, ("dp", "mp"), scatter_dimension=0, tiled=True),

time: 698 us -> 487 us (0.70)
  waiting for transfers between devices: 403 us -> 0 us
  Pallas kernels: 0 us -> 267 us
  matrix products: 121 us -> 101 us
  between operations: 15.2 us -> 1.79 us
  other arithmetic: 23.9 us -> 11.4 us
  starting transfers between devices: 10.3 us -> 0 us
  blocking collectives: 70.8 us -> 63.4 us
    pallas_call x0 -> x9, Pallas kernels: none -> 267 us  [the longest x1 140 us: sum_weights(): pl.pallas_call(functools.partial(weights_kernel, n), out_shape=[jax.Shape...]
    unnamed x8 -> x0, waiting for transfers between devices: 116 us -> none
    all_gather x4 -> x0, waiting for transfers between devices: 107 us -> none  [the longest x1 31.6 us: on_device(): gathered = lax.all_gather(normed, 'mp', axis=0, tiled=True)]
    reduce_scatter x2 -> x0, waiting for transfers between devices: 92.3 us -> none  [the longest x1 46.2 us: on_device(): lax.psum_scatter(jnp.einsum('tf,df->td', d_gate, w_gate, preferred_elemen...]
    all_to_all x2 -> x0, waiting for transfers between devices: 87.5 us -> none  [the longest x1 61.2 us: sent_and_summed(): lax.all_to_all(cut_along(shard, dim, length), axis, 0, 0, tiled=True)]
    unnamed x117 -> x132, local copies, waits for them, and re-layouts: 41.7 us -> 6.62 us
    convert_element_type x0 -> x3, local copies, waits for them, and re-layouts: none -> 25 us  [the longest x1 8.44 us: on_device(): up_part.astype(BF16)]
    all_to_all x2 -> x0, starting transfers between devices: 9.52 us -> none  [the longest x1 5.33 us: sent_and_summed(): lax.all_to_all(cut_along(shard, dim, length), axis, 0, 0, tiled=True)]
  transfers between devices with their start and end apart: 9 -> 0, of which waited for: 9 -> 0; matrix products, arithmetic and copies ran while one was open for 6% -> 0% of each run, Pallas kernels for 0% -> 0%
where the time goes in v1:
time: 487 us; the launch traced here: 484 us
  Pallas kernels  267 us (55%)
  matrix products  101 us (21%)
  blocking collectives  63.4 us (13%)
  local copies, waits for them, and re-layouts  39.3 us (8%)
  other arithmetic  11.4 us (2%)
    pallas_call x1, Pallas kernels, sum_weights(): pl.pallas_call(functools.partial(weights_kernel, n), out_shape=[jax.Shape...  140 us
    pallas_call x4, Pallas kernels, scatter_rows(): pl.pallas_call(scatter_kernel, out_shape=jax.ShapeDtypeStruct((tok, width...  64.3 us
    unnamed x1, blocking collectives  63.4 us
    pallas_call x4, Pallas kernels, gather_rows(): pl.pallas_call(gather_kernel, out_shape=jax.ShapeDtypeStruct((4 * tok, wi...  62.9 us
    dot_general x1, matrix products, mixer_block_back(): jnp.einsum('hts,htf->shf', d_raw_low, q_block, preferred_element_type=jnp...  11.7 us
    dot_general x1, matrix products, mixer_block_back(): jnp.einsum('hts,shf->htf', d_raw_low, key_rows, preferred_element_type=jn...  10.9 us

profile of v1, /device:TPU:1, one launch (start us, length us, event | category | flops | bytes accessed | tf_op | source)
XLA Modules:
  0.0 483.5 jit_solution(1237113763693998213)
XLA Ops:
  0.7 1.4 fusion.50
  2.6 1.2 fusion.43.own_ref
  3.8 16.8 %gather_rows.4 = bf16[512,2048]{1,0:T(8,128)(2,1)S(1)} custom-call(bf16[128,2048]{1,0:T(8,128)(2,1)S(1)} %fusion.43.own_ref), custom_call_target="tpu_custom_call" | custom-call | tf_op jit(solution)/shard_map/gather_rows/pallas_call | solution.py:101
  23.3 0.9 fusion.7
  24.2 2.4 fusion.3
  26.6 1.3 convolution_convert_fusion.8
  27.9 1.4 convolution_divide_fusion
  29.3 1.5 fusion.33
  30.8 1.3 fusion.77.part_ref
  32.1 15.9 %scatter_rows.4 = f32[128,2048]{1,0:T(8,128)S(1)} custom-call(f32[512,2048]{1,0:T(8,128)S(1)} %fusion.77.part_ref), custom_call_target="tpu_custom_call" | custom-call | tf_op jit(solution)/shard_map/scatter_rows/pallas_call | solution.py:158
  48.5 15.4 %gather_rows.5 = bf16[512,2048]{1,0:T(8,128)(2,1)S(1)} custom-call(bf16[128,2048]{1,0:T(8,128)(2,1)S(1)} %multiply_convert_fusion.3.own_ref), custom_call_target="tpu_custom_call" | custom-call | tf_op jit(solution)/shard_map/gather_rows/pallas_call | solution.py:101
  64.0 5.9 %fusion.78 = f32[512,1376]{0,1:T(8,128)S(1)} fusion(bf16[512,2048]{1,0:T(8,128)(2,1)S(1)} %gather_rows.5, bf16[2048,1376]{0,1:T(8,128)(2,1)} %param.20), kind=kOutput, calls=%fused_computation.107 | convolution fusion | flops 2885681152 | bytes 10551296 | tf_op jit(solution)/shard_map/dot_general | solution.py:541
  70.0 4.7 fusion.79
  74.7 15.3 %gather_rows.6 = bf16[512,2048]{1,0:T(8,128)(2,1)S(1)} custom-call(bf16[128,2048]{1,0:T(8,128)(2,1)S(1)} %bitcast.111), custom_call_target="tpu_custom_call" | custom-call | tf_op jit(solution)/shard_map/gather_rows/pallas_call | solution.py:101
  90.1 7.5 %multiply_convert_fusion = (bf16[512,1376]{0,1:T(8,128)(2,1)S(1)}, bf16[512,1376]{0,1:T(8,128)(2,1)S(1)}, bf16[512,1376]{0,1:T(8,128)(2,1)}) fusion(f32[512,1376]{0,1:T(8,128)S(1)} %fusion.78, f32[512,1376]{0,1:T(8,128)} %fusion.79, bf16[512,2048]{1,0:T(8,128)(2,1)S(1)} %gather_rows.6, bf16[1376,2048]{1,0:T(8,128)(2,1)S(1)} %bitcast.145), kind=kOutput, calls=%fused_computation.20 | convolution fusion | flops 2896248832 | bytes 17596416 | tf_op jit(solution)/shard_map/td,fd->tf/dot_general | solution.py:550
  97.6 3.5 fusion.81
  101.1 3.5 convolution_add_fusion.part_ref
  104.6 15.9 %scatter_rows.6 = f32[128,2048]{1,0:T(8,128)S(1)} custom-call(f32[512,2048]{1,0:T(8,128)S(1)} %convolution_add_fusion.part_ref), custom_call_target="tpu_custom_call" | custom-call | tf_op jit(solution)/shard_map/scatter_rows/pallas_call | solution.py:158
  120.5 0.9 multiply_reduce_fusion.1
  121.9 15.3 %gather_rows.7 = bf16[512,2048]{1,0:T(8,128)(2,1)S(1)} custom-call(bf16[128,2048]{1,0:T(8,128)(2,1)S(1)} %fusion.73.own_ref), custom_call_target="tpu_custom_call" | custom-call | tf_op jit(solution)/shard_map/gather_rows/pallas_call | solution.py:101
  137.3 1.3 fusion.42
  138.6 2.8 fusion.71
  141.4 2.8 fusion.82
  144.8 11.7 %fusion.38 = bf16[4,16,512]{2,1,0:T(8,128)(2,1)} fusion(bf16[4,512,16]{1,2,0:T(8,128)(2,1)S(1)} %bitcast.135, f32[4,512,512]{1,2,0:T(8,128)} %fusion.82, f32[4,512,512]{1,2,0:T(8,128)} %copy-done.17, f32[4,512,512]{1,2,0:T(8,128)} %fusion.71, f32[4,512]{1,0:T(4,128)} %get-tuple-element.101, f32[4,512]{1,0:T(4,128)} %get-tuple-element.102, ...), kind=kOutput, calls=%fused_computation.59 | convolution fusion | flops 51415552 | bytes 13254656 | tf_op jit(solution)/shard_map/while/body/eval_jaxpr/hts,htf->shf/dot_general | solution.py:482
  156.5 2.0 convolution_convert_fusion.5
  158.6 10.9 %fusion.35 = bf16[4,512,16]{1,2,0:T(8,128)(2,1)S(1)} fusion(bf16[512,4,16]{0,2,1:T(8,128)(2,1)S(1)} %bitcast.133, f32[4,512,512]{1,2,0:T(8,128)} %fusion.82, f32[4,512,512]{1,2,0:T(8,128)} %copy-done.17, f32[4,512,512]{1,2,0:T(8,128)} %fusion.71, f32[4,512]{1,0:T(4,128)} %get-tuple-element.101, f32[4,512]{1,0:T(4,128)} %get-tuple-element.102, ...), kind=kOutput, calls=%fused_computation.58 | convolution fusion | flops 51415552 | bytes 13254656 | tf_op jit(solution)/shard_map/while/body/eval_jaxpr/hts,shf->htf/dot_general | solution.py:479
  169.9 3.8 fusion.11
  173.8 1.2 fusion.34
  175.1 1.3 convolution_convert_fusion.3
  176.4 1.7 pad_maximum_fusion
  178.0 4.5 copy.64
  182.5 6.2 %convolution_convert_fusion.1 = bf16[2048,1376]{0,1:T(8,128)(2,1)} fusion(bf16[512,1376]{0,1:T(8,128)(2,1)} %copy-done.54, bf16[512,2048]{1,0:T(8,128)(2,1)S(1)} %copy-done.12), kind=kOutput, calls=%fused_computation.2 | convolution fusion | flops 2888499200 | bytes 9142272 | tf_op jit(solution)/shard_map/td,tf->df/dot_general | solution.py:556
  188.7 8.3 %copy.65 = bf16[2048,1376]{1,0:T(8,128)(2,1)} copy(bf16[2048,1376]{0,1:T(8,128)(2,1)} %convolution_convert_fusion.1) | data formatting | bytes 11272192 | tf_op jit(solution)/shard_map/convert_element_type | solution.py:606
  197.0 6.6 %convolution_convert_fusion = bf16[2048,1376]{0,1:T(8,128)(2,1)} fusion(bf16[512,1376]{0,1:T(8,128)(2,1)} %copy-done.26, bf16[512,2048]{1,0:T(8,128)(2,1)S(1)} %copy-done.12), kind=kOutput, calls=%fused_computation.1 | convolution fusion | flops 2888499200 | bytes 9142272 | tf_op jit(solution)/shard_map/td,tf->df/dot_general | solution.py:557
  203.6 8.4 %copy.66 = bf16[2048,1376]{1,0:T(8,128)(2,1)} copy(bf16[2048,1376]{0,1:T(8,128)(2,1)} %convolution_convert_fusion) | data formatting | bytes 11272192 | tf_op jit(solution)/shard_map/convert_element_type | solution.py:607
  212.0 3.8 convolution_convert_fusion.4
  215.8 4.9 %fusion.1 = bf16[2048,1376]{0,1:T(8,128)(2,1)} fusion(bf16[512,1376]{0,1:T(8,128)(2,1)S(1)} %copy-done.52, bf16[512,2048]{1,0:T(8,128)(2,1)S(1)} %copy-done.10), kind=kOutput, calls=%fused_computation.4 | convolution fusion | flops 2888499200 | bytes 9142272 | tf_op jit(solution)/shard_map/td,tf->df/dot_general | solution.py:555
  220.7 8.3 %copy.67 = bf16[2048,1376]{1,0:T(8,128)(2,1)} copy(bf16[2048,1376]{0,1:T(8,128)(2,1)} %fusion.1) | data formatting | bytes 11272192 | tf_op jit(solution)/shard_map/convert_element_type | solution.py:608
  229.0 139.5 %sum_weights.1 = (f32[64,640]{1,0:T(8,128)}, f32[64,512]{1,0:T(8,128)}, f32[64,1376]{1,0:T(8,128)}, f32[64,1376]{1,0:T(8,128)}, f32[64,1376]{1,0:T(8,128)}) custom-call(bf16[4,2,4,64,640]{4,3,2,1,0:T(8,128)(2,1)} %bitcast.115, bf16[4,2,4,64,512]{4,3,2,1,0:T(8,128)(2,1)} %bitcast.126, bf16[4,2,4,64,1376]{4,3,2,1,0:T(8,128)(2,1)} %bitcast.112, ...), custom_call_target="tpu_custom_call" | custom-call | tf_op jit(solution)/shard_map/sum_weights/pallas_call | solution.py:390
  368.6 1.7 slice.11
  370.3 1.5 fusion.76
  372.6 1.3 fusion.84
  374.8 16.4 %scatter_rows.7 = f32[128,2048]{1,0:T(8,128)S(1)} custom-call(f32[512,2048]{1,0:T(8,128)S(1)} %add_add_fusion.part_ref), custom_call_target="tpu_custom_call" | custom-call | tf_op jit(solution)/shard_map/scatter_rows/pallas_call | solution.py:158
  391.2 1.0 copy-done.5
  392.5 63.4 %all-reduce.2 = (f32[2048]{0:T(1024)S(1)}, f32[2048]{0:T(1024)S(1)}) all-reduce(f32[2048]{0:T(1024)S(1)} %get-tuple-element.82, f32[2048]{0:T(1024)S(1)} %copy-done.44), channel_id=2, replica_groups=mesh['dp'=32,'mp'=4] {'dp','mp'}, use_global_device_ids=true, to_apply=%region_12.13.clone | all-reduce | flops 4096 | bytes 32768
  457.1 5.4 %fusion.80.part_ref = f32[512,2048]{1,0:T(8,128)S(1)} fusion(bf16[512,1376]{0,1:T(8,128)(2,1)S(1)} %copy-done.53, bf16[1376,2048]{1,0:T(8,128)(2,1)} %param.22), kind=kOutput, calls=%fused_computation.109 | convolution fusion | flops 2885681152 | bytes 11239424 | tf_op jit(solution)/shard_map/dot_general | solution.py:546
  462.6 16.1 %scatter_rows.5 = f32[128,2048]{1,0:T(8,128)S(1)} custom-call(f32[512,2048]{1,0:T(8,128)S(1)} %fusion.80.part_ref), custom_call_target="tpu_custom_call" | custom-call | tf_op jit(solution)/shard_map/scatter_rows/pallas_call | solution.py:158
  478.9 1.6 fusion.48
  (151 shorter events, 11.4 us)
Async XLA Ops:
  0.6 30.2 %copy-start = (bf16[512,2048]{1,0:T(8,128)(2,1)S(1)}, bf16[512,2048]{1,0:T(8,128)(2,1)}, u32[]{:S(2)}) copy-start(bf16[512,2048]{1,0:T(8,128)(2,1)} %param.19) | copy-start | bytes 6291460
  0.7 20.0 %copy-start.29 = (bf16[2048,64]{0,1:T(8,128)(2,1)S(1)}, bf16[2048,64]{0,1:T(8,128)(2,1)}, u32[]{:S(2)}) copy-start(bf16[2048,64]{0,1:T(8,128)(2,1)} %param.16) | copy-start | bytes 786436
  0.7 21.3 %copy-start.31 = (bf16[2048,64]{0,1:T(8,128)(2,1)S(1)}, bf16[2048,64]{0,1:T(8,128)(2,1)}, u32[]{:S(2)}) copy-start(bf16[2048,64]{0,1:T(8,128)(2,1)} %param.17) | copy-start | bytes 786436
  2.6 20.1 %copy-start.51 = (s32[1,3]{1,0:T(1,128)S(1)}, s32[1,3]{1,0:T(1,128)}, u32[]{:S(2)}) copy-start(s32[1,3]{1,0:T(1,128)} %param.13) | copy-start | bytes 40
  23.3 4.6 copy-start.34
  24.2 5.1 %copy-start.17 = (f32[4,512,512]{1,2,0:T(8,128)}, f32[4,512,512]{1,2,0:T(8,128)S(1)}, u32[]{:S(2)}) copy-start(f32[4,512,512]{1,2,0:T(8,128)S(1)} %get-tuple-element.98) | copy-start | bytes 12582916
  30.8 17.2 %copy-start.36 = (bf16[4,512,128]{1,2,0:T(8,128)(2,1)}, bf16[4,512,128]{1,2,0:T(8,128)(2,1)S(1)}, u32[]{:S(2)}) copy-start(bf16[4,512,128]{1,2,0:T(8,128)(2,1)S(1)} %fusion.33) | copy-start | bytes 1572868
  32.1 15.9 %copy-start.19 = (bf16[1,128,2048]{2,1,0:T(8,128)(2,1)S(1)}, bf16[1,128,2048]{2,1,0:T(8,128)(2,1)}, u32[]{:S(2)}) copy-start(bf16[1,128,2048]{2,1,0:T(8,128)(2,1)} %param.12) | copy-start | bytes 1572868
  32.1 16.2 %copy-start.41 = (f32[2048]{0:T(1024)S(1)}, f32[2048]{0:T(1024)}, u32[]{:S(2)}) copy-start(f32[2048]{0:T(1024)} %param.15) | copy-start | bytes 24580
  48.3 73.1 %copy-start.15 = (f32[128,2048]{1,0:T(8,128)}, f32[128,2048]{1,0:T(8,128)S(1)}, u32[]{:S(2)}) copy-start(f32[128,2048]{1,0:T(8,128)S(1)} %get-tuple-element.87) | copy-start | bytes 3145732
  48.3 73.1 %copy-start.45 = (f32[128]{0:T(128)}, f32[128]{0:T(128)S(1)}, u32[]{:S(2)}) copy-start(f32[128]{0:T(128)S(1)} %add_rsqrt_fusion) | copy-start | bytes 1540
  48.5 21.4 %slice-start = ((s8[5636096]{0:T(1024)(128)(4,1)}), s8[4194304]{0:T(1024)(128)(4,1)S(1)}, s32[]{:S(2)}) async-start(s8[5636096]{0:T(1024)(128)(4,1)} %bitcast.116), calls=%async_computation | async-start | bytes 8388608
  63.9 6.0 %copy-start.11 = (bf16[512,2048]{1,0:T(8,128)(2,1)}, bf16[512,2048]{1,0:T(8,128)(2,1)S(1)}, u32[]{:S(2)}) copy-start(bf16[512,2048]{1,0:T(8,128)(2,1)S(1)} %gather_rows.5) | copy-start | bytes 6291460
  63.9 6.0 %slice-start.1 = ((s8[5636096]{0:T(1024)(128)(4,1)}), s8[1441792]{0:T(1024)(128)(4,1)S(1)}, s32[]{:S(2)}) async-start(s8[5636096]{0:T(1024)(128)(4,1)} %bitcast.116), calls=%async_computation.1 | async-start | bytes 2883584
  64.0 26.1 %slice-start.4 = ((s8[5636096]{0:T(1024)(128)(4,1)}), s8[4194304]{0:T(1024)(128)(4,1)S(1)}, s32[]{:S(2)}) async-start(s8[5636096]{0:T(1024)(128)(4,1)} %bitcast.144), calls=%async_computation.4 | async-start | bytes 8388608
  69.9 4.8 copy-start.7
  70.0 20.1 %slice-start.5 = ((s8[5636096]{0:T(1024)(128)(4,1)}), s8[1441792]{0:T(1024)(128)(4,1)S(1)}, s32[]{:S(2)}) async-start(s8[5636096]{0:T(1024)(128)(4,1)} %bitcast.144), calls=%async_computation.5 | async-start | bytes 2883584
  74.7 22.9 %slice-start.2 = ((s8[5636096]{0:T(1024)(128)(4,1)}), s8[4194304]{0:T(1024)(128)(4,1)S(1)}, s32[]{:S(2)}) async-start(s8[5636096]{0:T(1024)(128)(4,1)} %bitcast.142), calls=%async_computation.2 | async-start | bytes 8388608
  90.1 7.5 %copy-start.9 = (bf16[512,2048]{1,0:T(8,128)(2,1)}, bf16[512,2048]{1,0:T(8,128)(2,1)S(1)}, u32[]{:S(2)}) copy-start(bf16[512,2048]{1,0:T(8,128)(2,1)S(1)} %gather_rows.6) | copy-start | bytes 6291460
  90.1 7.6 %slice-start.3 = ((s8[5636096]{0:T(1024)(128)(4,1)}), s8[1441792]{0:T(1024)(128)(4,1)S(1)}, s32[]{:S(2)}) async-start(s8[5636096]{0:T(1024)(128)(4,1)} %bitcast.142), calls=%async_computation.3 | async-start | bytes 2883584
  97.6 3.5 copy-start.26
  120.5 16.8 %copy-start.56 = (f32[4,512,128]{1,2,0:T(8,128)S(1)}, f32[4,512,128]{1,2,0:T(8,128)}, u32[]{:S(2)}) copy-start(f32[4,512,128]{1,2,0:T(8,128)} %copy-done.55) | copy-start | bytes 3145732
  137.3 4.1 copy-start.13
  138.6 5.6 %copy-start.22 = (bf16[512,512]{0,1:T(8,128)(2,1)}, bf16[512,512]{0,1:T(8,128)(2,1)S(1)}, u32[]{:S(2)}) copy-start(bf16[512,512]{0,1:T(8,128)(2,1)S(1)} %get-tuple-element.100) | copy-start | bytes 1572868
  144.8 11.7 %copy-start.4 = (bf16[512,2048]{1,0:T(8,128)(2,1)S(1)}, bf16[512,2048]{1,0:T(8,128)(2,1)}, u32[]{:S(2)}) copy-start(bf16[512,2048]{1,0:T(8,128)(2,1)} %copy-done.2) | copy-start | bytes 6291460
  169.4 4.3 copy-start.18
  169.4 4.3 copy-start.23
  169.4 4.3 copy-start.35
  176.4 6.2 %copy-start.12 = (bf16[512,2048]{1,0:T(8,128)(2,1)S(1)}, bf16[512,2048]{1,0:T(8,128)(2,1)}, u32[]{:S(2)}) copy-start(bf16[512,2048]{1,0:T(8,128)(2,1)} %copy-done.11) | copy-start | bytes 6291460
  203.6 8.4 %copy-start.14 = (bf16[512,2048]{1,0:T(8,128)(2,1)S(1)}, bf16[512,2048]{1,0:T(8,128)(2,1)}, u32[]{:S(2)}) copy-start(bf16[512,2048]{1,0:T(8,128)(2,1)} %copy-done.13) | copy-start | bytes 6291460
  212.0 3.8 copy-start.10
  212.0 3.8 copy-start.52
  229.0 142.8 %copy-start.30 = (bf16[2048,64]{0,1:T(8,128)(2,1)S(1)}, bf16[2048,64]{0,1:T(8,128)(2,1)}, u32[]{:S(2)}) copy-start(bf16[2048,64]{0,1:T(8,128)(2,1)} %param.16) | copy-start | bytes 786436
  368.6 4.0 copy-start.25
  368.6 4.0 copy-start.28
  374.7 17.4 %copy-start.20 = (bf16[1,128,2048]{2,1,0:T(8,128)(2,1)S(1)}, bf16[1,128,2048]{2,1,0:T(8,128)(2,1)}, u32[]{:S(2)}) copy-start(bf16[1,128,2048]{2,1,0:T(8,128)(2,1)} %param.12) | copy-start | bytes 1572868
  374.7 17.4 %copy-start.43 = (f32[2048]{0:T(1024)S(1)}, f32[2048]{0:T(1024)}, u32[]{:S(2)}) copy-start(f32[2048]{0:T(1024)} %param.14) | copy-start | bytes 24580
  374.7 17.4 %copy-start.48 = (f32[128]{0:T(128)S(1)}, f32[128]{0:T(128)}, u32[]{:S(2)}) copy-start(f32[128]{0:T(128)} %copy-done.47) | copy-start | bytes 1540
  374.8 17.8 %copy-start.44 = (f32[2048]{0:T(1024)S(1)}, f32[2048]{0:T(1024)}, u32[]{:S(2)}) copy-start(f32[2048]{0:T(1024)} %get-tuple-element.80) | copy-start | bytes 24580
  374.8 82.3 %copy-start.53 = (bf16[512,1376]{0,1:T(8,128)(2,1)S(1)}, bf16[512,1376]{0,1:T(8,128)(2,1)}, u32[]{:S(2)}) copy-start(bf16[512,1376]{0,1:T(8,128)(2,1)} %get-tuple-element.90) | copy-start | bytes 4227076
  462.5 16.2 %copy-start.6 = (f32[128,2048]{1,0:T(8,128)S(1)}, f32[128,2048]{1,0:T(8,128)}, u32[]{:S(2)}) copy-start(f32[128,2048]{1,0:T(8,128)} %copy-done.5) | copy-start | bytes 3145732
  462.5 16.2 %copy-start.8 = (bf16[1,128,2048]{2,1,0:T(8,128)(2,1)S(1)}, bf16[1,128,2048]{2,1,0:T(8,128)(2,1)}, u32[]{:S(2)}) copy-start(bf16[1,128,2048]{2,1,0:T(8,128)(2,1)} %param.23) | copy-start | bytes 1572868
  462.6 16.2 %copy-start.16 = (f32[128,2048]{1,0:T(8,128)S(1)}, f32[128,2048]{1,0:T(8,128)}, u32[]{:S(2)}) copy-start(f32[128,2048]{1,0:T(8,128)} %copy-done.15) | copy-start | bytes 3145732
  462.6 16.2 %copy-start.21 = (bf16[1,128,2048]{2,1,0:T(8,128)(2,1)S(1)}, bf16[1,128,2048]{2,1,0:T(8,128)(2,1)}, u32[]{:S(2)}) copy-start(bf16[1,128,2048]{2,1,0:T(8,128)(2,1)} %param.12) | copy-start | bytes 1572868
  462.6 16.2 %copy-start.46 = (f32[128]{0:T(128)S(1)}, f32[128]{0:T(128)}, u32[]{:S(2)}) copy-start(f32[128]{0:T(128)} %copy-done.45) | copy-start | bytes 1540
  462.6 16.2 %copy-start.50 = (f32[128]{0:T(128)S(1)}, f32[128]{0:T(128)}, u32[]{:S(2)}) copy-start(f32[128]{0:T(128)} %copy-done.49) | copy-start | bytes 1540
  462.6 20.7 %copy-start.1 = (bf16[512,2048]{1,0:T(8,128)(2,1)S(1)}, bf16[512,2048]{1,0:T(8,128)(2,1)}, u32[]{:S(2)}) copy-start(bf16[512,2048]{1,0:T(8,128)(2,1)} %param.19) | copy-start | bytes 6291460
  478.8 3.8 copy-start.37
  (15 other events, 27.2 us)
